TPU v7x, 1024 devices: a whole 8x8x8 slice. The times are simulated.
1024 devices in a mesh: fsdp: 32 (over x, y_lo, core), head: 32 (over y_hi, z).
Axes of the slice: x: 8, y: 8 (y_hi: 4, y_lo: 2; y = y_hi * 2 + y_lo), z: 8, core: 2. Of those that a mesh axis runs over, the one named last changes fastest.
Arguments:
- query_nope: float32 [8192, 16384], P('fsdp', 'head'), may hold values from -6 to 6
- query_rope: float32 [8192, 8192], P('fsdp', 'head'), may hold values from -12 to 12
- latent: float32 [8192, 512], P(('fsdp', 'head')), may hold values from -6 to 6
- rope_key: float32 [8192, 64], P(('fsdp', 'head')), may hold values from -4 to 4
- cotangent: float32 [8192, 16384], P('fsdp', 'head'), may hold values from -6 to 6
- bounds: int32 [32, 2], P('fsdp'), may hold values from 1 to 256, as said below
- key_up: float32 [512, 16384], P('fsdp', 'head'), may hold values from -0.25 to 0.25
- value_up: float32 [512, 16384], P('fsdp', 'head'), may hold values from -0.25 to 0.25
Outputs:
- query_nope_grad: float32 [8192, 16384], P('fsdp', 'head')
- query_rope_grad: float32 [8192, 8192], P('fsdp', 'head')
- latent_grad: float32 [8192, 512], P(('fsdp', 'head'))
- rope_key_grad: float32 [8192, 64], P(('fsdp', 'head'))
- key_up_grad: float32 [512, 16384], P('fsdp', 'head')
- value_up_grad: float32 [512, 16384], P('fsdp', 'head')
Inputs may be any that keep to these rules, and one draw needn't show every extreme that they name: bounds[s, 0] is the length of sequence s's image prefix, attended in both directions, and bounds[s, 1] its number of valid tokens; 1 <= bounds[s, 0] < 128 < bounds[s, 1]; some sequence has all 256 tokens valid.
All inputs are finite; a program needn't handle non-finite values.
Results may differ from a plain program's by a relative error of at most 0.0003.
Values sent between devices are 32-bit elements; how exact they have to be, the bound alone decides.
A program may use at most 32 MiB of HBM per device.

v0:
```python
import jax
import jax.numpy as jnp
from jax import lax
from jax.sharding import PartitionSpec as P

NOPE = 128
ROPE = 64
VHEAD = 128


HIGHEST = lax.Precision.HIGHEST


def sent_together(arrays, axis, dim, along):
    both = jnp.concatenate(arrays, axis=along)
    filled, at, gathered = (lax.all_gather(both, axis, axis=dim, tiled=True), 0, [])
    for a in arrays:
        gathered.append(lax.slice_in_dim(filled, at, at + a.shape[along], axis=along))
        at += a.shape[along]
    return tuple(gathered)


def in_blocks(shard, dim, peers):
    lengths = shard.shape
    blocks = shard.reshape(*lengths[:dim], peers, lengths[dim] // peers, *lengths[dim + 1 :])
    return jnp.moveaxis(blocks, dim, 0)


def sent_and_summed(shard, axis, dim):
    peers = lax.axis_size(axis)
    blocks = lax.all_to_all(in_blocks(shard, dim, peers), axis, 0, 0, tiled=True)
    return jnp.sum(blocks, axis=0)


def side_by_side(arrays, axis, dim, along):
    both = jnp.concatenate(arrays, axis=along)
    filled, at, gathered = (sent_and_summed(both, axis, dim), 0, [])
    for a in arrays:
        gathered.append(lax.slice_in_dim(filled, at, at + a.shape[along], axis=along))
        at += a.shape[along]
    return tuple(gathered)


def visible_mask(limits, length):
    position = jnp.arange(length)
    query_pos = position[:, None]
    key_pos = position[None, :]
    return (key_pos < limits[1]) & ((key_pos <= query_pos) | (key_pos < limits[0]))


def attention_grads(query_nope, query_rope, key_rows, value_rows, shared_rows, cotangent, limits):
    length = query_nope.shape[0]
    head_count = query_nope.shape[1] // NOPE
    query_nope = query_nope.reshape(length, head_count, NOPE)
    query_rope = query_rope.reshape(length, head_count, ROPE)
    key_rows = key_rows.reshape(length, head_count, NOPE)
    value_rows = value_rows.reshape(length, head_count, VHEAD)
    cotangent = cotangent.reshape(length, head_count, VHEAD)
    factor = (NOPE + ROPE) ** (-0.5)
    scores = jnp.einsum("ihd,jhd->hij", query_nope, key_rows, precision=HIGHEST)
    scores = (
        scores + jnp.einsum("ihr,jr->hij", query_rope, shared_rows, precision=HIGHEST)
    ) * factor
    scores = jnp.where(visible_mask(limits, length)[None], scores, -jnp.inf)
    attend = jax.nn.softmax(scores, axis=-1)
    outputs = jnp.einsum("hij,jhv->ihv", attend, value_rows, precision=HIGHEST)
    row_dot = jnp.sum(cotangent * outputs, axis=-1)
    value_grad = jnp.einsum("hij,ihv->jhv", attend, cotangent, precision=HIGHEST)
    grad_attend = jnp.einsum("ihv,jhv->hij", cotangent, value_rows, precision=HIGHEST)
    grad_scores = attend * (grad_attend - jnp.transpose(row_dot)[:, :, None]) * factor
    nope_grad = jnp.einsum("hij,jhd->ihd", grad_scores, key_rows, precision=HIGHEST)
    rope_grad = jnp.einsum("hij,jr->ihr", grad_scores, shared_rows, precision=HIGHEST)
    key_grad = jnp.einsum("hij,ihd->jhd", grad_scores, query_nope, precision=HIGHEST)
    shared_grad = jnp.einsum("hij,ihr->jr", grad_scores, query_rope, precision=HIGHEST)
    return (
        nope_grad.reshape(length, head_count * NOPE),
        rope_grad.reshape(length, head_count * ROPE),
        key_grad.reshape(length, head_count * NOPE),
        value_grad.reshape(length, head_count * VHEAD),
        shared_grad,
    )


def matmul(left, right):
    return jnp.dot(left, right, precision=HIGHEST, preferred_element_type=jnp.float32)


def contract_rows(left, right):
    return lax.dot_general(
        left, right, (((0,), (0,)), ((), ())), precision=HIGHEST, preferred_element_type=jnp.float32
    )


def contract_columns(left, right):
    return lax.dot_general(
        left, right, (((1,), (1,)), ((), ())), precision=HIGHEST, preferred_element_type=jnp.float32
    )


def on_device(query_nope, query_rope, latent, rope_key, cotangent, bounds, key_up, value_up):
    latent_full, shared_full = sent_together((latent, rope_key), "head", 0, 1)
    limits = bounds[0]
    key_full, value_full = sent_together((key_up, value_up), "fsdp", 0, 1)
    key_rows = matmul(latent_full, key_full)
    value_rows = matmul(latent_full, value_full)
    nope_grad, rope_grad, key_grad, value_grad, shared_grad = attention_grads(
        query_nope, query_rope, key_rows, value_rows, shared_full, cotangent, limits
    )
    latent_term = contract_columns(key_grad, key_full) + contract_columns(value_grad, value_full)
    latent_grad, rope_key_grad = side_by_side((latent_term, shared_grad), "head", 0, 1)
    joined = jnp.concatenate([key_grad, value_grad], axis=1)
    both_grads = sent_and_summed(contract_rows(latent_full, joined), "fsdp", 0)
    split_at = key_grad.shape[1]
    key_up_grad = both_grads[:, :split_at]
    value_up_grad = both_grads[:, split_at:]
    return (nope_grad, rope_grad, latent_grad, rope_key_grad, key_up_grad, value_up_grad)


def solution(mesh):
    return jax.shard_map(
        on_device,
        mesh=mesh,
        in_specs=(
            P("fsdp", "head"),
            P("fsdp", "head"),
            P(("fsdp", "head"), None),
            P(("fsdp", "head"), None),
            P("fsdp", "head"),
            P("fsdp", None),
            P("fsdp", "head"),
            P("fsdp", "head"),
        ),
        out_specs=(
            P("fsdp", "head"),
            P("fsdp", "head"),
            P(("fsdp", "head"), None),
            P(("fsdp", "head"), None),
            P("fsdp", "head"),
            P("fsdp", "head"),
        ),
        check_vma=False,
    )
```

profile of v0, /device:TPU:1, one launch (start us, length us, event | category | flops | bytes accessed | tf_op | source)
XLA Modules:
  0.0 221.1 jit_solution(12272561653774946865)
XLA Ops:
  7.2 0.0 copy-start.3
  7.2 0.0 copy-start.7
  7.2 0.0 copy-start.6
  7.2 0.0 copy-start.5
  7.2 0.0 all-gather.2.cloned.1.call-start
  7.3 1.5 pad_maximum_fusion
  8.7 0.0 all-gather.2.cloned.1.call-update
  8.7 1.1 copy.58
  9.8 1.2 copy.84
  11.1 0.0 copy-done.3
  11.1 0.2 copy.59
  11.3 0.6 fusion.32
  11.9 1.3 iota_compare_fusion.1
  13.2 0.0 copy-done.6
  13.2 0.0 copy-done.5
  13.2 0.8 fusion.25
  14.0 86.4 %all_gather.6 = f32[256,576]{1,0:T(8,128)S(1)} all-gather(f32[8,576]{1,0:T(8,128)S(1)} %pad_maximum_fusion.1), channel_id=1, replica_groups=mesh['fsdp'=32,'head'=32] {'head'}, dimensions={0}, use_global_device_ids=true | all-gather | bytes 608256 | tf_op jit(solution)/shard_map/all_gather | solution.py:16
  100.3 1.0 convolution_bitcast_fusion
  101.3 0.0 all-gather.2.cloned.1.call-done
  101.3 0.0 copy-start.4
  101.3 3.1 %fusion.17 = f32[256,512]{0,1:T(8,128)S(1)} fusion(f32[512,1024]{1,0:T(8,128)} %all-gather.2.cloned.1.call-done, f32[256,576]{1,0:T(8,128)S(1)} %all_gather.6), kind=kOutput, calls=%fused_computation.24 | convolution fusion | flops 805306368 | bytes 2097152 | tf_op jit(solution)/shard_map/dot_general | solution.py:85
  104.4 1.1 fusion.33
  105.6 0.2 fusion.20
  105.8 1.4 fusion.28
  107.1 0.2 copy-done
  107.3 1.8 fusion.13
  109.2 0.9 fusion.7
  110.1 1.2 fusion.2
  111.2 1.0 convolution_bitcast_fusion.3
  112.2 1.2 fusion.35
  113.4 2.0 fusion.15
  115.5 1.9 convolution_add_fusion
  117.4 0.0 copy-start.2
  117.4 0.9 maximum_bitcast_fusion
  118.3 5.2 %all-to-all-start = ((f32[32,8,576]{2,1,0:T(8,128)}), f32[32,8,576]{2,1,0:T(8,128)}, u32[]{:S(2)}, u32[]{:S(2)}) async-start(f32[32,8,576]{2,1,0:T(8,128)} %maximum_bitcast_fusion), calls=%async_computation | async-start | bytes 1310720 | tf_op jit(solution)/shard_map/all_to_all | solution.py:31
  123.5 4.8 %fusion.8 = f32[512,1024]{1,0:T(8,128)} fusion(f32[256,512]{0,1:T(8,128)S(1)} %bitcast.79, f32[256,512]{0,1:T(8,128)S(1)} %bitcast.75, f32[256,576]{1,0:T(8,128)S(1)} %all_gather.6), kind=kOutput, calls=%fused_computation.14 | convolution fusion | flops 1610874880 | bytes 3670016 | tf_op jit(solution)/shard_map/dot_general | solution.py:89
  128.3 9.0 %all-to-all-done = f32[32,8,576]{2,1,0:T(8,128)} async-done(((f32[32,8,576]{2,1,0:T(8,128)}), f32[32,8,576]{2,1,0:T(8,128)}, u32[]{:S(2)}, u32[]{:S(2)}) %all-to-all-start) | async-done | bytes 589856 | tf_op jit(solution)/shard_map/all_to_all | solution.py:31
  137.3 24.5 %all-to-all-start.1 = ((f32[32,16,1024]{2,1,0:T(8,128)}), f32[32,16,1024]{2,1,0:T(8,128)}, u32[]{:S(2)}, u32[]{:S(2)}) async-start(f32[32,16,1024]{2,1,0:T(8,128)} %bitcast.69), calls=%async_computation.1 | async-start | bytes 4194304 | tf_op jit(solution)/shard_map/all_to_all | solution.py:31
  161.8 0.8 fusion.26
  162.6 0.8 copy.73
  163.4 0.8 fusion.34
  164.2 1.0 copy.72
  165.2 1.1 reduce_sum.38
  166.3 0.6 slice.47
  166.9 0.6 slice.46
  167.5 44.4 %all-to-all-done.1 = f32[32,16,1024]{2,1,0:T(8,128)} async-done(((f32[32,16,1024]{2,1,0:T(8,128)}), f32[32,16,1024]{2,1,0:T(8,128)}, u32[]{:S(2)}, u32[]{:S(2)}) %all-to-all-start.1) | async-done | bytes 2097184 | tf_op jit(solution)/shard_map/all_to_all | solution.py:31
  211.9 1.7 reduce_sum.39
  213.6 0.6 fusion.31
  (7 shorter events, 0.0 us)
Async XLA Ops:
  7.2 3.9 %copy-start.3 = (f32[256,512]{1,0:T(8,128)S(1)}, f32[256,512]{1,0:T(8,128)}, u32[]{:S(2)}) copy-start(f32[256,512]{1,0:T(8,128)} %param.12) | copy-start | bytes 1572868
  7.2 4.1 %copy-start.7 = (s32[1,2]{1,0:T(1,128)S(1)}, s32[1,2]{1,0:T(1,128)}, u32[]{:S(2)}) copy-start(s32[1,2]{1,0:T(1,128)} %param.13) | copy-start | bytes 28
  7.2 6.0 %copy-start.6 = (f32[8,64]{1,0:T(8,128)S(1)}, f32[8,64]{1,0:T(8,128)}, u32[]{:S(2)}) copy-start(f32[8,64]{1,0:T(8,128)} %param.11) | copy-start | bytes 6148
  7.2 6.0 %copy-start.5 = (f32[8,512]{1,0:T(8,128)S(1)}, f32[8,512]{1,0:T(8,128)}, u32[]{:S(2)}) copy-start(f32[8,512]{1,0:T(8,128)} %param.10) | copy-start | bytes 49156
  7.2 94.1 %all-gather.2.cloned.1.call-start = ((), (), s32[]{:S(2)}) async-start(), calls=%async_computation.2 | async-start | bytes 2162688 | tf_op jit(solution)/shard_map/all_gather | solution.py:16
  101.3 3.1 %copy-start.4 = (pred[256,256]{0,1:T(8,128)(4,1)S(1)}, pred[256,256]{0,1:T(8,128)(4,1)}, u32[]{:S(2)}) copy-start(pred[256,256]{0,1:T(8,128)(4,1)} %fusion.25) | copy-start | bytes 196612
  105.7 1.6 copy-start
  107.3 8.2 %copy-start.1 = (f32[4,256,128]{1,2,0:T(8,128)}, f32[4,256,128]{1,2,0:T(8,128)S(1)}, u32[]{:S(2)}) copy-start(f32[4,256,128]{1,2,0:T(8,128)S(1)} %fusion.28) | copy-start | bytes 1572868
  117.4 6.1 %copy-start.2 = (f32[4,256,128]{1,2,0:T(8,128)S(1)}, f32[4,256,128]{1,2,0:T(8,128)}, u32[]{:S(2)}) copy-start(f32[4,256,128]{1,2,0:T(8,128)} %copy-done.1) | copy-start | bytes 1572868
  118.3 19.0 %all-to-all-start = ((f32[32,8,576]{2,1,0:T(8,128)}), f32[32,8,576]{2,1,0:T(8,128)}, u32[]{:S(2)}, u32[]{:S(2)}) async-start(f32[32,8,576]{2,1,0:T(8,128)} %maximum_bitcast_fusion), calls=%async_computation | async-start | bytes 1310720 | tf_op jit(solution)/shard_map/all_to_all | solution.py:31
  137.3 74.6 %all-to-all-start.1 = ((f32[32,16,1024]{2,1,0:T(8,128)}), f32[32,16,1024]{2,1,0:T(8,128)}, u32[]{:S(2)}, u32[]{:S(2)}) async-start(f32[32,16,1024]{2,1,0:T(8,128)} %bitcast.69), calls=%async_computation.1 | async-start | bytes 4194304 | tf_op jit(solution)/shard_map/all_to_all | solution.py:31
Sparse Core Ops, SparseCore 0:
  11.3 82.3 all-gather.1
where the time goes:
time: 222 us; the launch traced here: 221 us
  blocking collectives  86.4 us (39%)
  waiting for transfers between devices  53.4 us (24%)
  starting transfers between devices  29.7 us (13%)
  matrix products  22.8 us (10%)
  between operations  14.3 us (6%)
  other arithmetic  7.44 us (3%)
  local copies, waits for them, and re-layouts  7.01 us (3%)
    all_gather x1, blocking collectives, sent_together(): lax.all_gather(both, axis, axis=dim, tiled=True)  86.4 us
    all_to_all x2, waiting for transfers between devices, sent_and_summed(): lax.all_to_all(in_blocks(shard, dim, peers), axis, 0, 0, tiled=True)  53.4 us
    all_to_all x2, starting transfers between devices, sent_and_summed(): lax.all_to_all(in_blocks(shard, dim, peers), axis, 0, 0, tiled=True)  29.7 us
    dot_general x2, matrix products, matmul(): jnp.dot(left, right, precision=HIGHEST, preferred_element_type=jnp.float32)  4.87 us
    dot_general x1, matrix products, contract_rows(): lax.dot_general(left, right, (((0,), (0,)), ((), ())), precision=HIGHEST,...  4.8 us
  transfers between devices with their start and end apart: 3, of which 2 were waited for; matrix products, arithmetic and copies ran while one was open for 8% of the time, Pallas kernels for 0%

commit v1 on v0

v1 whole, which is shorter than its diff:
```python
import jax
import jax.numpy as jnp
from jax import lax
from jax.experimental import pallas as pl
from jax.experimental.pallas import tpu as pltpu
from jax.sharding import PartitionSpec as P

NOPE = 128
ROPE = 64
VHEAD = 128
SEQ = 256
LAT = 512
LANES = 640
HEADS_HERE = 4
MESH = pl.DeviceIdType.MESH
F32 = jnp.float32
HIGH = lax.Precision.HIGH
FACTOR = (NOPE + ROPE) ** (-0.5)

NX, NYL, NC, NYH, NZ = 8, 2, 2, 4, 8


def dot_nn(a, b):
    return lax.dot_general(a, b, (((1,), (0,)), ((), ())), precision=HIGH, preferred_element_type=F32)


def dot_nt(a, b):
    return lax.dot_general(a, b, (((1,), (1,)), ((), ())), precision=HIGH, preferred_element_type=F32)


class Sems:
    def __init__(self, send, recv):
        self.send, self.recv, self.used = send, recv, 0

    def next(self):
        at = self.used
        self.used += 1
        return self.send.at[at], self.recv.at[at]


N_SEMS = 120


def kernel(
    qn_hbm, qr_hbm, lat_hbm, rk_hbm, cot_hbm, bounds_ref, ku_hbm, vu_hbm,
    qng_hbm, qrg_hbm, lg_hbm, rkg_hbm, kug_hbm, vug_hbm,
    qn, qr, cot, rk, wb, lb, latt, qng, qrg,
    ugb, sb, pb, yb, qb, xr3, xr4, xr1, xr2,
    lgb, zr3, zr4, zr1, zr2, lacc, yr, lgo, rkgo, kugo, vugo,
    send, recv, local,
):
    f = lax.axis_index("fsdp")
    hd = lax.axis_index("head")
    x, y, c = f // 4, (f // 2) % 2, f % 2
    yh, z = hd // NZ, hd % NZ
    sgn = 1 - 2 * c

    def fx(dx):
        return (((x + dx + 2 * NX) % NX * NYL + y) * NC + c, hd)

    to_y = ((x * NYL + (1 - y)) * NC + c, hd)
    to_sib = ((x * NYL + y) * NC + (1 - c), hd)

    def hz(dz):
        return (f, yh * NZ + (z + dz + 2 * NZ) % NZ)

    def hy(r):
        return (f, (yh + r) % NYH * NZ + z)

    def xi(dx):
        return (x + dx + 2 * NX) % NX

    def zi(dz):
        return (z + dz + 2 * NZ) % NZ

    sems = Sems(send, recv)

    def fetch(src, dst, k):
        cp = pltpu.make_async_copy(src, dst, local.at[k])
        cp.start()
        return cp

    c_ku = fetch(ku_hbm, wb.at[f, :, pl.ds(0, 512)], 0)
    c_vu = fetch(vu_hbm, wb.at[f, :, pl.ds(512, 512)], 1)
    c_la = fetch(lat_hbm, lb.at[0, z, :, pl.ds(0, LAT)], 2)
    c_rk = fetch(rk_hbm, rk, 3)
    c_qn = fetch(qn_hbm, qn, 4)
    c_qr = fetch(qr_hbm, qr, 5)
    c_co = fetch(cot_hbm, cot, 6)

    partners = [fx(1), fx(-1), fx(2), fx(-2), to_y, to_sib, hz(1), hz(-1), hz(2), hz(-2), hy(1), hy(2), hy(3)]
    barrier = pltpu.get_barrier_semaphore()
    for p in partners:
        pl.semaphore_signal(barrier, inc=1, device_id=p, device_id_type=MESH)

    c_ku.wait()
    c_vu.wait()
    c_rk.wait()
    c_la.wait()
    lb[0, z, :, pl.ds(LAT, 128)] = jnp.concatenate([rk[...], jnp.zeros((8, 64), F32)], axis=1)
    pl.semaphore_wait(barrier, len(partners))

    started = []

    def push(src, dst, dev):
        s, r = sems.next()
        cp = pltpu.make_async_remote_copy(
            src_ref=src, dst_ref=dst, send_sem=s, recv_sem=r, device_id=dev, device_id_type=MESH
        )
        cp.start()
        started.append(cp)
        return cp

    def wsl(dx, yy, cc):
        return wb.at[(xi(dx) * NYL + yy) * NC + cc]

    def same(ref, dev):
        return push(ref, ref, dev)

    own_w = wsl(0, y, c)
    own_l = lb.at[0, z]

    def lb_r(r):
        return lb.at[r, z]

    ly = [push(own_l, lb_r(NYH - r), hy(r)) for r in (1, 2, 3)]
    xa = {}
    za = {}
    za[2] = same(own_l, hz(2))
    za[-2] = same(own_l, hz(-2))
    xa[2] = same(own_w, fx(2))
    xa[-2] = same(own_w, fx(-2))
    za[1] = same(own_l, hz(1))
    za[-1] = same(own_l, hz(-1))
    ya = {0: same(own_w, to_y)}
    xa[1] = same(own_w, fx(1))
    xa[-1] = same(own_w, fx(-1))
    sa = {("x", 0): same(own_w, to_sib)}

    for cp in ly:
        cp.wait_recv()
    rest = lb.at[pl.ds(1, 3), z]
    zb = {d: same(rest, hz(d)) for d in (2, -2, 1, -1)}

    for d in (1, -1):
        xa[d].wait_recv()
        ya[-d] = same(wsl(-d, y, c), to_y)
        sa[("x", -d)] = same(wsl(-d, y, c), to_sib)
    ya[0].wait_recv()
    sa[("y", 0)] = same(wsl(0, 1 - y, c), to_sib)
    for d in (2, -2):
        xa[d].wait_recv()
        xa[d + d // 2] = same(wsl(-d, y, c), fx(d // 2))
    xa[4] = same(wsl(-2 * sgn, y, c), fx(2 * sgn))
    for d in (2, -2):
        ya[-d] = same(wsl(-d, y, c), to_y)
        sa[("x", -d)] = same(wsl(-d, y, c), to_sib)
    for d in (2, -2):
        za[d].wait_recv()
        zb[d].wait_recv()
        za[d + d // 2] = same(lb.at[:, zi(-d)], hz(d // 2))
    za[4] = same(lb.at[:, zi(-2 * sgn)], hz(2 * sgn))
    for d in (1, -1):
        ya[d].wait_recv()
        sa[("y", d)] = same(wsl(d, 1 - y, c), to_sib)
    for d in (3, -3):
        xa[d].wait_recv()
        ya[-d] = same(wsl(-d, y, c), to_y)
        sa[("x", -d)] = same(wsl(-d, y, c), to_sib)
    xa[4].wait_recv()
    ya[4] = same(wsl(4, y, c), to_y)
    sa[("x", 4)] = same(wsl(4, y, c), to_sib)
    for d in (2, -2):
        ya[d].wait_recv()
        sa[("y", d)] = same(wsl(d, 1 - y, c), to_sib)
    for d in (1, -1):
        za[d].wait_recv()
        zb[d].wait_recv()
    for d in (3, -3, 4):
        za[d].wait_recv()
    for d in (3, -3, 4):
        ya[d].wait_recv()
        sa[("y", d)] = same(wsl(d, 1 - y, c), to_sib)
    c_qn.wait()
    c_qr.wait()
    c_co.wait()

    lat = lb[:, :, :, pl.ds(0, LAT)].reshape(SEQ, LAT)
    rope = lb[:, :, :, pl.ds(LAT, 128)].reshape(SEQ, 128)[:, :ROPE]
    latt[...] = lat.T
    for cp in sa.values():
        cp.wait_recv()

    row = lax.broadcasted_iota(jnp.int32, (SEQ, SEQ), 0)
    query = lax.broadcasted_iota(jnp.int32, (SEQ, SEQ), 1)
    turned = row + yh * 64
    key = jnp.where(turned >= SEQ, turned - SEQ, turned)
    visible = (key < bounds_ref[0, 1]) & ((key <= query) | (key < bounds_ref[0, 0]))

    def kv_up(h):
        a = wb[:, :, pl.ds(h * NOPE, NOPE)].reshape(LAT, NOPE)
        b = wb[:, :, pl.ds(512 + h * VHEAD, VHEAD)].reshape(LAT, VHEAD)
        return jnp.concatenate([a, b], axis=1)

    s1, s2, s3, s4, s5 = {}, {}, {}, {}, {}

    def stage1(h):
        s1[h] = push(ugb.at[h, :, 1 - c], sb.at[h], to_sib)

    def stage2(h):
        s1[h].wait_recv()
        pb[h] = ugb[h, :, pl.ds(c, 1)].reshape(8, 2, 16, 256) + sb[h].reshape(8, 2, 16, 256)
        s2[h] = push(pb.at[h, :, 1 - y], yb.at[h], to_y)

    def stage3(h):
        s2[h].wait_recv()
        qb[h] = pb[h, :, pl.ds(y, 1)].reshape(8, 16, 256) + yb[h]
        s3[h] = (
            push(qb.at[h, xi(3)], xr3.at[h, 0], fx(1)),
            push(qb.at[h, xi(-3)], xr3.at[h, 1], fx(-1)),
            push(qb.at[h, xi(4)], xr4.at[h], fx(2 * sgn)),
        )
        s4[h] = [
            push(qb.at[h, xi(1)], xr1.at[h, 0], fx(1)),
            push(qb.at[h, xi(-1)], xr1.at[h, 1], fx(-1)),
        ]

    def stage4(h):
        for cp in s3[h]:
            cp.wait_recv()
        xr2_own = [qb[h, xi(2)] + xr3[h, 0], qb[h, xi(-2)] + xr3[h, 1]]
        qb[h, xi(2)] = xr2_own[0]
        qb[h, xi(-2)] = xr2_own[1]
        qb[h, xi(2 * sgn)] = qb[h, xi(2 * sgn)] + xr4[h]
        s4[h] += [
            push(qb.at[h, xi(2)], xr2.at[h, 0], fx(2)),
            push(qb.at[h, xi(-2)], xr2.at[h, 1], fx(-2)),
        ]

    def stage5(h):
        for cp in s4[h]:
            cp.wait_recv()
        total = qb[h, x] + (xr1[h, 0] + xr1[h, 1]) + (xr2[h, 0] + xr2[h, 1])
        kugo[:, pl.ds(h * NOPE, NOPE)] = total[:, :NOPE]
        vugo[:, pl.ds(h * VHEAD, VHEAD)] = total[:, NOPE:]

    shared = None
    latent_term = None
    outs = []
    rope_grads = []
    for h in range(HEADS_HERE):
        up = kv_up(h)
        kv = dot_nn(lat, up)
        kk = jnp.concatenate([kv[:, :NOPE], rope], axis=1)
        vv = kv[:, NOPE:]
        q = jnp.concatenate([qn[:, pl.ds(h * NOPE, NOPE)], qr[:, h * ROPE : (h + 1) * ROPE]], axis=1)
        ct = cot[:, pl.ds(h * VHEAD, VHEAD)]
        scores = dot_nt(kk, q) * FACTOR
        scores = jnp.where(visible, scores, -jnp.inf)
        top = jnp.max(scores, axis=0, keepdims=True)
        attend = jnp.exp(scores - top)
        attend = attend / jnp.sum(attend, axis=0, keepdims=True)
        grad_attend = dot_nt(vv, ct)
        row_dot = jnp.sum(attend * grad_attend, axis=0, keepdims=True)
        grad_scores = attend * (grad_attend - row_dot) * FACTOR
        vg = dot_nn(attend, ct)
        kg = dot_nn(grad_scores, q)
        qg = dot_nn(grad_scores.T, kk)
        qng[:, pl.ds(h * NOPE, NOPE)] = qg[:, :NOPE]
        rope_grads.append(qg[:, NOPE:])
        shared = kg[:, NOPE:] if shared is None else shared + kg[:, NOPE:]
        both = jnp.concatenate([kg[:, :NOPE], vg], axis=1)
        term = dot_nt(both, up)
        latent_term = term if latent_term is None else latent_term + term
        if h == HEADS_HERE - 1:
            lgb[:, :, :, pl.ds(0, LAT)] = latent_term.reshape(NYH, NZ, 8, LAT)
            lgb[:, :, :, pl.ds(LAT, 128)] = jnp.concatenate(
                [shared, jnp.zeros((SEQ, 64), F32)], axis=1
            ).reshape(NYH, NZ, 8, 128)
            l3 = (
                push(lgb.at[:, zi(3)], zr3.at[0], hz(1)),
                push(lgb.at[:, zi(-3)], zr3.at[1], hz(-1)),
                push(lgb.at[:, zi(4)], zr4, hz(2 * sgn)),
            )
            l1 = [
                push(lgb.at[:, zi(1)], zr1.at[0], hz(1)),
                push(lgb.at[:, zi(-1)], zr1.at[1], hz(-1)),
            ]
        ugb[h] = dot_nn(latt[...], both).reshape(16, 2, 16, 256)
        stage1(h)
        if h % 2 == 1:
            qrg[:, pl.ds((h - 1) * ROPE, 128)] = jnp.concatenate(rope_grads[-2:], axis=1)
        if h >= 1:
            stage2(h - 1)
        if h >= 2:
            stage3(h - 2)
        if h >= 3:
            stage4(h - 3)

    def put(src, dst, k):
        cp = pltpu.make_async_copy(src, dst, local.at[k])
        cp.start()
        outs.append(cp)

    put(qng, qng_hbm, 7)
    put(qrg, qrg_hbm, 8)
    stage2(3)
    stage3(2)
    stage4(1)
    stage5(0)
    for cp in l3:
        cp.wait_recv()
    lgb[:, pl.ds(zi(2), 1)] = lgb[:, pl.ds(zi(2), 1)] + zr3[0].reshape(NYH, 1, 8, LANES)
    lgb[:, pl.ds(zi(-2), 1)] = lgb[:, pl.ds(zi(-2), 1)] + zr3[1].reshape(NYH, 1, 8, LANES)
    lgb[:, pl.ds(zi(2 * sgn), 1)] = lgb[:, pl.ds(zi(2 * sgn), 1)] + zr4[...].reshape(NYH, 1, 8, LANES)
    l1 += [
        push(lgb.at[:, zi(2)], zr2.at[0], hz(2)),
        push(lgb.at[:, zi(-2)], zr2.at[1], hz(-2)),
    ]
    stage3(3)
    stage4(2)
    stage5(1)
    for cp in l1:
        cp.wait_recv()
    lacc[...] = (
        lgb[:, pl.ds(z, 1)].reshape(NYH, 8, LANES) + (zr1[0] + zr1[1]) + (zr2[0] + zr2[1])
    )
    l4 = [push(lacc.at[r], yr.at[r - 1], hy(r)) for r in (1, 2, 3)]
    stage4(3)
    stage5(2)
    for cp in l4:
        cp.wait_recv()
    total = (lacc[0] + yr[0]) + (yr[1] + yr[2])
    lgo[...] = total[:, :LAT]
    rkgo[...] = total[:, LAT : LAT + ROPE]
    put(lgo, lg_hbm, 9)
    put(rkgo, rkg_hbm, 10)
    stage5(3)
    put(kugo, kug_hbm, 11)
    put(vugo, vug_hbm, 12)
    for cp in started:
        cp.wait_send()
    for cp in outs:
        cp.wait()


def hand_over(*refs):
    for a, b in zip(refs[:6], refs[6:]):
        b[...] = a[...]


def on_device(query_nope, query_rope, latent, rope_key, cotangent, bounds, key_up, value_up):
    shapes = [
        (SEQ, 512), (SEQ, 256), (8, LAT), (8, ROPE), (16, 512), (16, 512),
    ]
    out_shape = [jax.ShapeDtypeStruct(s, F32) for s in shapes]
    hbm = pl.BlockSpec(memory_space=pl.ANY)
    vm = lambda *s: pltpu.VMEM(s, F32)
    results = pl.pallas_call(
        kernel,
        out_shape=out_shape,
        in_specs=[hbm] * 5 + [pl.BlockSpec(memory_space=pltpu.SMEM)] + [hbm] * 2,
        out_specs=[hbm] * 6,
        scratch_shapes=[
            vm(SEQ, 512), vm(SEQ, 256), vm(SEQ, 512), vm(8, ROPE),
            vm(32, 16, 1024), vm(NYH, NZ, 8, LANES), vm(LAT, SEQ), vm(SEQ, 512), vm(SEQ, 256),
            vm(4, 16, 2, 16, 256), vm(4, 16, 16, 256), vm(4, 8, 2, 16, 256), vm(4, 8, 16, 256),
            vm(4, 8, 16, 256), vm(4, 2, 16, 256), vm(4, 16, 256), vm(4, 2, 16, 256), vm(4, 2, 16, 256),
            vm(NYH, NZ, 8, LANES), vm(2, NYH, 8, LANES), vm(NYH, 8, LANES),
            vm(2, NYH, 8, LANES), vm(2, NYH, 8, LANES), vm(NYH, 8, LANES), vm(3, 8, LANES),
            vm(8, LAT), vm(8, ROPE), vm(16, 512), vm(16, 512),
            pltpu.SemaphoreType.DMA((N_SEMS,)),
            pltpu.SemaphoreType.DMA((N_SEMS,)),
            pltpu.SemaphoreType.DMA((13,)),
        ],
        compiler_params=pltpu.CompilerParams(
            collective_id=0, has_side_effects=True, vmem_limit_bytes=60 * 2**20
        ),
        name="fused",
    )(query_nope, query_rope, latent, rope_key, cotangent, bounds, key_up, value_up)
    whole = pl.BlockSpec(memory_space=pltpu.VMEM)
    return pl.pallas_call(
        hand_over,
        out_shape=out_shape,
        in_specs=[whole] * 6,
        out_specs=[whole] * 6,
        compiler_params=pltpu.CompilerParams(vmem_limit_bytes=60 * 2**20),
        name="hand_over",
    )(*results)


def solution(mesh):
    return jax.shard_map(
        on_device,
        mesh=mesh,
        in_specs=(
            P("fsdp", "head"),
            P("fsdp", "head"),
            P(("fsdp", "head"), None),
            P(("fsdp", "head"), None),
            P("fsdp", "head"),
            P("fsdp", None),
            P("fsdp", "head"),
            P("fsdp", "head"),
        ),
        out_specs=(
            P("fsdp", "head"),
            P("fsdp", "head"),
            P(("fsdp", "head"), None),
            P(("fsdp", "head"), None),
            P("fsdp", "head"),
            P("fsdp", "head"),
        ),
        check_vma=False,
    )
```

time: 222 us -> 72.1 us (0.32)
  blocking collectives: 86.4 us -> 0 us
  Pallas kernels: 0 us -> 70.8 us
  waiting for transfers between devices: 53.4 us -> 0 us
  starting transfers between devices: 29.7 us -> 0 us
  matrix products: 22.8 us -> 0 us
  between operations: 14.3 us -> 0.64 us
  other arithmetic: 7.44 us -> 0 us
  local copies, waits for them, and re-layouts: 7.01 us -> 0 us
    all_gather x1 -> x0, blocking collectives: 86.4 us -> none  [sent_together(): lax.all_gather(both, axis, axis=dim, tiled=True)]
    pallas_call x0 -> x2, Pallas kernels: none -> 70.8 us  [the longest x1 68.8 us: on_device(): pl.pallas_call(kernel, out_shape=out_shape, in_specs=[hbm] * 5 + [pl.Bloc...]
    all_to_all x2 -> x0, waiting for transfers between devices: 53.4 us -> none  [sent_and_summed(): lax.all_to_all(in_blocks(shard, dim, peers), axis, 0, 0, tiled=True)]
    all_to_all x2 -> x0, starting transfers between devices: 29.7 us -> none  [sent_and_summed(): lax.all_to_all(in_blocks(shard, dim, peers), axis, 0, 0, tiled=True)]
    dot_general x14 -> x0, matrix products: 22.8 us -> none  [the longest x2 4.87 us: matmul(): jnp.dot(left, right, precision=HIGHEST, preferred_element_type=jnp.float32)]
    unnamed x20 -> x0, local copies, waits for them, and re-layouts: 3.36 us -> none
    reduce_sum x3 -> x0, other arithmetic: 3.01 us -> none  [the longest x2 2.85 us: sent_and_summed(): return jnp.sum(blocks, axis=0)]
    slice x4 -> x0, local copies, waits for them, and re-layouts: 2.42 us -> none  [the longest x2 1.2 us: side_by_side(): lax.slice_in_dim(filled, at, at + a.shape[along], axis=along)]
  transfers between devices with their start and end apart: 3 -> 0, of which waited for: 2 -> 0; matrix products, arithmetic and copies ran while one was open for 8% -> 0% of each run, Pallas kernels for 0% -> 0%
where the time goes in v1:
time: 72.1 us; the launch traced here: 71.5 us
  Pallas kernels  70.8 us (98%)
    pallas_call x1, Pallas kernels, on_device(): pl.pallas_call(kernel, out_shape=out_shape, in_specs=[hbm] * 5 + [pl.Bloc...  68.8 us
    pallas_call x1, Pallas kernels, on_device(): pl.pallas_call(hand_over, out_shape=out_shape, in_specs=[whole] * 6, out_...  2.05 us

profile of v1, /device:TPU:1, one launch (start us, length us, event | category | flops | bytes accessed | tf_op | source)
XLA Modules:
  0.0 71.5 jit_solution(6630182126312895149)
XLA Ops:
  0.6 68.8 %fused.1 = (f32[256,512]{1,0:T(8,128)}, f32[256,256]{1,0:T(8,128)}, f32[8,512]{1,0:T(8,128)}, f32[8,64]{1,0:T(8,128)}, f32[16,512]{1,0:T(8,128)}, /*index=5*/f32[16,512]{1,0:T(8,128)}) custom-call(f32[256,512]{1,0:T(8,128)} %qn_hbm.1, f32[256,256]{1,0:T(8,128)} %qr_hbm.1, f32[8,512]{1,0:T(8,128)} %lat_hbm.1, f32[8,64]{1,0:T(8,128)} %rk_hbm.1, ...), custom_call_target="tpu_custom_call" | custom-call | tf_op jit(solution)/shard_map/fused/pallas_call | solution.py:359
  69.4 2.1 %hand_over.1 = (f32[256,512]{1,0:T(8,128)}, f32[256,256]{1,0:T(8,128)}, f32[8,512]{1,0:T(8,128)}, f32[8,64]{1,0:T(8,128)}, f32[16,512]{1,0:T(8,128)}, /*index=5*/f32[16,512]{1,0:T(8,128)}) custom-call(f32[256,512]{1,0:T(8,128)} %get-tuple-element.12.refs_0_, f32[256,256]{1,0:T(8,128)} %get-tuple-element.13.refs_1_, f32[8,512]{1,0:T(8,128)} %get-tuple-element.14.refs_2_, ...), custom_call_target="tpu_custom_call" | custom-call | tf_op jit(solution)/shard_map/hand_over/pallas_call | solution.py:382

commit v2 on v0

v2 whole, which is shorter than its diff:
```python
import jax
import jax.numpy as jnp
from jax import lax
from jax.experimental import pallas as pl
from jax.experimental.pallas import tpu as pltpu
from jax.sharding import PartitionSpec as P

NOPE = 128
ROPE = 64
VHEAD = 128
SEQ = 256
LAT = 512
LANES = 640
HEADS_HERE = 4
MESH = pl.DeviceIdType.MESH
F32 = jnp.float32
HIGH = lax.Precision.HIGH
FACTOR = (NOPE + ROPE) ** (-0.5)

NX, NYL, NC, NYH, NZ = 8, 2, 2, 4, 8


def dot_nn(a, b):
    return lax.dot_general(a, b, (((1,), (0,)), ((), ())), precision=HIGH, preferred_element_type=F32)


def dot_nt(a, b):
    return lax.dot_general(a, b, (((1,), (1,)), ((), ())), precision=HIGH, preferred_element_type=F32)


N_SEMS = 128


def kernel(
    qn_hbm, qr_hbm, lat_hbm, rk_hbm, cot_hbm, bounds_ref, ku_hbm, vu_hbm,
    qng_hbm, qrg_hbm, lg_hbm, rkg_hbm, kug_hbm, vug_hbm,
    qn, qr, cot, rk, wb, lb, latt, qng, qrg,
    ugb, sb, pb, yb, qb, xr,
    lgb, zr3, zr4, zr1, zr2, lacc, yr, lgo, rkgo, kugo, vugo,
    send, recv, local,
):
    f = lax.axis_index("fsdp")
    hd = lax.axis_index("head")
    x, y, c = f // 4, (f // 2) % 2, f % 2
    yh, z = hd // NZ, hd % NZ
    sgn = 1 - 2 * c

    def xi(dx):
        return (x + dx + 2 * NX) % NX

    def zi(dz):
        return (z + dz + 2 * NZ) % NZ

    def fx(dx):
        return ((xi(dx) * NYL + y) * NC + c, hd)

    def hz(dz):
        return (f, yh * NZ + zi(dz))

    def hy(r):
        return (f, (yh + r) % NYH * NZ + z)

    to_y = ((x * NYL + (1 - y)) * NC + c, hd)
    to_sib = ((x * NYL + y) * NC + (1 - c), hd)
    around = (2, -2, 3, -3, 4, 1, -1)

    n_local = [0]

    def on_device_copy(src, dst):
        cp = pltpu.make_async_copy(src, dst, local.at[n_local[0]])
        n_local[0] += 1
        cp.start()
        return cp

    started = []

    def push(src, dst, dev):
        k = len(started)
        cp = pltpu.make_async_remote_copy(
            src_ref=src, dst_ref=dst, send_sem=send.at[k], recv_sem=recv.at[k], device_id=dev, device_id_type=MESH
        )
        cp.start()
        started.append(cp)
        return cp

    def same(ref, dev):
        return push(ref, ref, dev)

    def landed(copies):
        for cp in copies:
            cp.wait_recv()

    own = [on_device_copy(lat_hbm, lb.at[0, z, :, pl.ds(0, LAT)]), on_device_copy(rk_hbm, rk)]
    for h in range(HEADS_HERE):
        own.append(on_device_copy(ku_hbm.at[:, pl.ds(h * NOPE, NOPE)], wb.at[h, x, y, c, :, pl.ds(0, NOPE)]))
        own.append(on_device_copy(vu_hbm.at[:, pl.ds(h * VHEAD, VHEAD)], wb.at[h, x, y, c, :, pl.ds(NOPE, VHEAD)]))
    later = [on_device_copy(qn_hbm, qn), on_device_copy(qr_hbm, qr), on_device_copy(cot_hbm, cot)]

    partners = [fx(d) for d in around] + [to_y, to_sib] + [hz(d) for d in around] + [hy(r) for r in (1, 2, 3)]
    barrier = pltpu.get_barrier_semaphore()
    for p in partners:
        pl.semaphore_signal(barrier, inc=1, device_id=p, device_id_type=MESH)
    for cp in own:
        cp.wait()
    lb[0, z, :, pl.ds(LAT, 128)] = jnp.concatenate([rk[...], jnp.zeros((8, 64), F32)], axis=1)
    pl.semaphore_wait(barrier, len(partners))

    ly = {r: push(lb.at[0, z], lb.at[NYH - r, z], hy(r)) for r in (1, 3, 2)}
    za = {d: same(lb.at[0, z], hz(d)) for d in around}
    xa, ya, sx, sy = {}, {}, {}, {}
    for h in range(HEADS_HERE):
        xa[h] = [same(wb.at[h, x, y, c], fx(d)) for d in around]
    zb = {d: [] for d in around}
    for r in (1, 3, 2):
        ly[r].wait_recv()
        for d in (2, -2, 1, -1):
            zb[d].append(same(lb.at[NYH - r, z], hz(d)))

    def row_over(h):
        landed(xa[h])
        ya[h] = same(wb.at[h, :, y, c], to_y)
        sx[h] = same(wb.at[h, :, y, c], to_sib)

    def other_row_over(h):
        ya[h].wait_recv()
        sy[h] = same(wb.at[h, :, 1 - y, c], to_sib)

    row_over(0)
    for d in (2, -2):
        landed(zb[d])
        zb[d + d // 2].append(same(lb.at[pl.ds(1, 3), zi(-d)], hz(d // 2)))
    zb[4].append(same(lb.at[pl.ds(1, 3), zi(-2 * sgn)], hz(2 * sgn)))
    row_over(1)
    other_row_over(0)
    row_over(2)
    for d in around:
        za[d].wait_recv()
    landed(zb[1] + zb[-1])
    landed(zb[3] + zb[-3] + zb[4])
    for cp in later:
        cp.wait()

    lat = lb[:, :, :, pl.ds(0, LAT)].reshape(SEQ, LAT)
    rope = lb[:, :, :, pl.ds(LAT, 128)].reshape(SEQ, 128)[:, :ROPE]

    row = lax.broadcasted_iota(jnp.int32, (SEQ, SEQ), 0)
    query = lax.broadcasted_iota(jnp.int32, (SEQ, SEQ), 1)
    turned = row + yh * 64
    key = jnp.where(turned >= SEQ, turned - SEQ, turned)
    visible = (key < bounds_ref[0, 1]) & ((key <= query) | (key < bounds_ref[0, 0]))

    s1, s2, s3 = {}, {}, {}

    def stage1(h):
        ugb[h] = dot_nn(latt[...], both[h]).reshape(16, 2, 16, 256)
        s1[h] = push(ugb.at[h, :, 1 - c], sb.at[h], to_sib)

    def stage2(h):
        s1[h].wait_recv()
        pb[h] = ugb[h, :, pl.ds(c, 1)].reshape(8, 2, 16, 256) + sb[h].reshape(8, 2, 16, 256)
        s2[h] = push(pb.at[h, :, 1 - y], yb.at[h], to_y)

    def stage3(h):
        s2[h].wait_recv()
        qb[h] = pb[h, :, pl.ds(y, 1)].reshape(8, 16, 256) + yb[h]
        s3[h] = [push(qb.at[h, xi(d)], xr.at[h, k], fx(d)) for k, d in enumerate(around)]

    def stage4(h):
        landed(s3[h])
        total = (qb[h, x] + xr[h, 0]) + (xr[h, 1] + xr[h, 2])
        total = total + ((xr[h, 3] + xr[h, 4]) + (xr[h, 5] + xr[h, 6]))
        kugo[:, pl.ds(h * NOPE, NOPE)] = total[:, :NOPE]
        vugo[:, pl.ds(h * VHEAD, VHEAD)] = total[:, NOPE:]

    both = {}
    rope_grads = []
    shared = latent_term = None
    for h in range(HEADS_HERE):
        landed([sx[h], sy[h]])
        up = wb[h].reshape(LAT, 256)
        kv = dot_nn(lat, up)
        if h == 0:
            latt[...] = lat.T
        kk = jnp.concatenate([kv[:, :NOPE], rope], axis=1)
        vv = kv[:, NOPE:]
        q = jnp.concatenate([qn[:, pl.ds(h * NOPE, NOPE)], qr[:, h * ROPE : (h + 1) * ROPE]], axis=1)
        ct = cot[:, pl.ds(h * VHEAD, VHEAD)]
        scores = dot_nt(kk, q) * FACTOR
        scores = jnp.where(visible, scores, -jnp.inf)
        top = jnp.max(scores, axis=0, keepdims=True)
        attend = jnp.exp(scores - top)
        attend = attend * (1.0 / jnp.sum(attend, axis=0, keepdims=True))
        grad_attend = dot_nt(vv, ct)
        row_dot = jnp.sum(attend * grad_attend, axis=0, keepdims=True)
        grad_scores = attend * (grad_attend - row_dot) * FACTOR
        vg = dot_nn(attend, ct)
        kg = dot_nn(grad_scores, q)
        qg = dot_nn(grad_scores.T, kk)
        qng[:, pl.ds(h * NOPE, NOPE)] = qg[:, :NOPE]
        rope_grads.append(qg[:, NOPE:])
        shared = kg[:, NOPE:] if shared is None else shared + kg[:, NOPE:]
        both[h] = jnp.concatenate([kg[:, :NOPE], vg], axis=1)
        if h % 2 == 1:
            qrg[:, pl.ds((h - 1) * ROPE, 128)] = jnp.concatenate(rope_grads[-2:], axis=1)
        if h == 0:
            row_over(3)
        if h < 3:
            other_row_over(h + 1)
        term = dot_nt(both[h], up)
        latent_term = term if latent_term is None else latent_term + term
        if h < 3:
            if h > 0:
                stage2(h - 1)
            stage1(h)

    lgb[pl.ds(0, 3), :, :, pl.ds(0, LAT)] = latent_term[64:].reshape(3, NZ, 8, LAT)
    lgb[3, :, :, pl.ds(0, LAT)] = latent_term[:64].reshape(NZ, 8, LAT)
    shared = jnp.concatenate([shared, jnp.zeros((SEQ, 64), F32)], axis=1)
    lgb[pl.ds(0, 3), :, :, pl.ds(LAT, 128)] = shared[64:].reshape(3, NZ, 8, 128)
    lgb[3, :, :, pl.ds(LAT, 128)] = shared[:64].reshape(NZ, 8, 128)
    l3, l1 = {}, {}
    for g in (0, 1):
        part = pl.ds(2 * g, 2)
        l3[g] = [
            push(lgb.at[part, zi(4)], zr4.at[part], hz(2 * sgn)),
            push(lgb.at[part, zi(3)], zr3.at[0, part], hz(1)),
            push(lgb.at[part, zi(-3)], zr3.at[1, part], hz(-1)),
        ]
        l1[g] = [
            push(lgb.at[part, zi(1)], zr1.at[0, part], hz(1)),
            push(lgb.at[part, zi(-1)], zr1.at[1, part], hz(-1)),
        ]

    def latent_step2(g):
        landed(l3[g])
        part = pl.ds(2 * g, 2)
        for k, d in enumerate((2, -2)):
            at = (part, pl.ds(zi(d), 1))
            lgb[at] = lgb[at] + zr3[k, part].reshape(2, 1, 8, LANES)
        at = (part, pl.ds(zi(2 * sgn), 1))
        lgb[at] = lgb[at] + zr4[part].reshape(2, 1, 8, LANES)
        l1[g] += [push(lgb.at[part, zi(d)], zr2.at[k, part], hz(d)) for k, d in enumerate((2, -2))]

    l4 = []

    def latent_step3(g):
        landed(l1[g])
        part = pl.ds(2 * g, 2)
        lacc[part] = (
            lgb[part, pl.ds(z, 1)].reshape(2, 8, LANES) + (zr1[0, part] + zr1[1, part]) + (zr2[0, part] + zr2[1, part])
        )
        for p in (2 * g + 1, 2 * g):
            if p < 3:
                l4.append(push(lacc.at[p], yr.at[p], hy(p + 1)))

    outs = []
    stage1(3)
    stage2(2)
    stage3(0)
    stage2(3)
    outs.append(on_device_copy(qng, qng_hbm))
    outs.append(on_device_copy(qrg, qrg_hbm))
    stage3(1)
    latent_step2(0)
    stage3(2)
    latent_step2(1)
    stage3(3)
    latent_step3(0)
    latent_step3(1)
    stage4(0)
    stage4(1)
    stage4(2)
    landed(l4)
    total = (lacc[3] + yr[0]) + (yr[1] + yr[2])
    lgo[...] = total[:, :LAT]
    rkgo[...] = total[:, LAT : LAT + ROPE]
    outs.append(on_device_copy(lgo, lg_hbm))
    outs.append(on_device_copy(rkgo, rkg_hbm))
    stage4(3)
    outs.append(on_device_copy(kugo, kug_hbm))
    outs.append(on_device_copy(vugo, vug_hbm))
    assert len(started) <= N_SEMS and n_local[0] <= 20
    for cp in started:
        cp.wait_send()
    for cp in outs:
        cp.wait()


def hand_over(*refs):
    sem = refs[12]
    copies = [pltpu.make_async_copy(a, b, sem.at[i]) for i, (a, b) in enumerate(zip(refs[:6], refs[6:12]))]
    for cp in copies:
        cp.start()
    for cp in copies:
        cp.wait()


def on_device(query_nope, query_rope, latent, rope_key, cotangent, bounds, key_up, value_up):
    shapes = [
        (SEQ, 512), (SEQ, 256), (8, LAT), (8, ROPE), (16, 512), (16, 512),
    ]
    out_shape = [jax.ShapeDtypeStruct(s, F32) for s in shapes]
    hbm = pl.BlockSpec(memory_space=pltpu.HBM)
    free = pl.BlockSpec(memory_space=pl.ANY)
    vm = lambda *s: pltpu.VMEM(s, F32)
    results = pl.pallas_call(
        kernel,
        out_shape=out_shape,
        in_specs=[hbm] * 5 + [pl.BlockSpec(memory_space=pltpu.SMEM)] + [hbm] * 2,
        out_specs=[free] * 6,
        scratch_shapes=[
            vm(SEQ, 512), vm(SEQ, 256), vm(SEQ, 512), vm(8, ROPE),
            vm(4, 8, 2, 2, 16, 256), vm(NYH, NZ, 8, LANES), vm(LAT, SEQ), vm(SEQ, 512), vm(SEQ, 256),
            vm(4, 16, 2, 16, 256), vm(4, 16, 16, 256), vm(4, 8, 2, 16, 256), vm(4, 8, 16, 256),
            vm(4, 8, 16, 256), vm(4, 7, 16, 256),
            vm(NYH, NZ, 8, LANES), vm(2, NYH, 8, LANES), vm(NYH, 8, LANES),
            vm(2, NYH, 8, LANES), vm(2, NYH, 8, LANES), vm(NYH, 8, LANES), vm(3, 8, LANES),
            vm(8, LAT), vm(8, ROPE), vm(16, 512), vm(16, 512),
            pltpu.SemaphoreType.DMA((N_SEMS,)),
            pltpu.SemaphoreType.DMA((N_SEMS,)),
            pltpu.SemaphoreType.DMA((20,)),
        ],
        compiler_params=pltpu.CompilerParams(
            collective_id=0, has_side_effects=True, vmem_limit_bytes=40 * 2**20
        ),
        name="fused",
    )(*[
        pltpu.with_memory_space_constraint(a, pltpu.HBM)
        for a in (query_nope, query_rope, latent, rope_key, cotangent, bounds, key_up, value_up)
    ])
    return pl.pallas_call(
        hand_over,
        out_shape=out_shape,
        in_specs=[free] * 6,
        out_specs=[hbm] * 6,
        scratch_shapes=[pltpu.SemaphoreType.DMA((6,))],
        compiler_params=pltpu.CompilerParams(vmem_limit_bytes=2 * 2**20),
        name="hand_over",
    )(*results)


def solution(mesh):
    return jax.shard_map(
        on_device,
        mesh=mesh,
        in_specs=(
            P("fsdp", "head"),
            P("fsdp", "head"),
            P(("fsdp", "head"), None),
            P(("fsdp", "head"), None),
            P("fsdp", "head"),
            P("fsdp", None),
            P("fsdp", "head"),
            P("fsdp", "head"),
        ),
        out_specs=(
            P("fsdp", "head"),
            P("fsdp", "head"),
            P(("fsdp", "head"), None),
            P(("fsdp", "head"), None),
            P("fsdp", "head"),
            P("fsdp", "head"),
        ),
        check_vma=False,
    )
```

time: 222 us -> 66.9 us (0.30)
  blocking collectives: 86.4 us -> 0 us
  Pallas kernels: 0 us -> 66 us
  waiting for transfers between devices: 53.4 us -> 0 us
  starting transfers between devices: 29.7 us -> 0 us
  matrix products: 22.8 us -> 0 us
  between operations: 14.3 us -> 0.64 us
  other arithmetic: 7.44 us -> 0 us
  local copies, waits for them, and re-layouts: 7.01 us -> 0 us
    all_gather x1 -> x0, blocking collectives: 86.4 us -> none  [sent_together(): lax.all_gather(both, axis, axis=dim, tiled=True)]
    pallas_call x0 -> x2, Pallas kernels: none -> 66 us  [the longest x1 65.1 us: on_device(): pl.pallas_call(kernel, out_shape=out_shape, in_specs=[hbm] * 5 + [pl.Bloc...]
    all_to_all x2 -> x0, waiting for transfers between devices: 53.4 us -> none  [sent_and_summed(): lax.all_to_all(in_blocks(shard, dim, peers), axis, 0, 0, tiled=True)]
    all_to_all x2 -> x0, starting transfers between devices: 29.7 us -> none  [sent_and_summed(): lax.all_to_all(in_blocks(shard, dim, peers), axis, 0, 0, tiled=True)]
    dot_general x14 -> x0, matrix products: 22.8 us -> none  [the longest x2 4.87 us: matmul(): jnp.dot(left, right, precision=HIGHEST, preferred_element_type=jnp.float32)]
    unnamed x20 -> x0, local copies, waits for them, and re-layouts: 3.36 us -> none
    reduce_sum x3 -> x0, other arithmetic: 3.01 us -> none  [the longest x2 2.85 us: sent_and_summed(): return jnp.sum(blocks, axis=0)]
    slice x4 -> x0, local copies, waits for them, and re-layouts: 2.42 us -> none  [the longest x2 1.2 us: side_by_side(): lax.slice_in_dim(filled, at, at + a.shape[along], axis=along)]
  transfers between devices with their start and end apart: 3 -> 0, of which waited for: 2 -> 0; matrix products, arithmetic and copies ran while one was open for 8% -> 0% of each run, Pallas kernels for 0% -> 0%
where the time goes in v2:
time: 66.9 us; the launch traced here: 66.7 us
  Pallas kernels  66 us (99%)
    pallas_call x1, Pallas kernels, on_device(): pl.pallas_call(kernel, out_shape=out_shape, in_specs=[hbm] * 5 + [pl.Bloc...  65.1 us

profile of v2, /device:TPU:1, one launch (start us, length us, event | category | flops | bytes accessed | tf_op | source)
XLA Modules:
  0.0 66.7 jit_solution(8437446793098120283)
XLA Ops:
  0.6 65.1 %fused.1 = (f32[256,512]{1,0:T(8,128)S(1)}, f32[256,256]{1,0:T(8,128)S(1)}, f32[8,512]{1,0:T(8,128)S(1)}, f32[8,64]{1,0:T(8,128)S(1)}, f32[16,512]{1,0:T(8,128)S(1)}, /*index=5*/f32[16,512]{1,0:T(8,128)S(1)}) custom-call(f32[256,512]{1,0:T(8,128)} %qn_hbm.1, f32[256,256]{1,0:T(8,128)} %qr_hbm.1, f32[8,512]{1,0:T(8,128)} %lat_hbm.1, f32[8,64]{1,0:T(8,128)} %rk_hbm.1, ...), custom_call_target="tpu_custom_call" | custom-call | tf_op jit(solution)/shard_map/fused/pallas_call | solution.py:306
  65.7 0.9 %hand_over.1 = (f32[256,512]{1,0:T(8,128)}, f32[256,256]{1,0:T(8,128)}, f32[8,512]{1,0:T(8,128)}, f32[8,64]{1,0:T(8,128)}, f32[16,512]{1,0:T(8,128)}, /*index=5*/f32[16,512]{1,0:T(8,128)}) custom-call(f32[256,512]{1,0:T(8,128)S(1)} %get-tuple-element.12.refs_0_, f32[256,256]{1,0:T(8,128)S(1)} %get-tuple-element.13.refs_1_, ...), custom_call_target="tpu_custom_call" | custom-call | tf_op jit(solution)/shard_map/hand_over/pallas_call | solution.py:331

commit v3 on v2

--- a/solution.py
+++ b/solution.py
@@ -140,6 +140,8 @@
     for cp in later:
         cp.wait()
 
+    row_over(3)
+    other_row_over(1)
     lat = lb[:, :, :, pl.ds(0, LAT)].reshape(SEQ, LAT)
     rope = lb[:, :, :, pl.ds(LAT, 128)].reshape(SEQ, 128)[:, :ROPE]
 
@@ -186,6 +188,10 @@
         q = jnp.concatenate([qn[:, pl.ds(h * NOPE, NOPE)], qr[:, h * ROPE : (h + 1) * ROPE]], axis=1)
         ct = cot[:, pl.ds(h * VHEAD, VHEAD)]
         scores = dot_nt(kk, q) * FACTOR
+        if h > 0:
+            term = dot_nt(both[h - 1], up_before)
+            latent_term = term if latent_term is None else latent_term + term
+            ugb[h - 1] = dot_nn(latt[...], both[h - 1]).reshape(16, 2, 16, 256)
         scores = jnp.where(visible, scores, -jnp.inf)
         top = jnp.max(scores, axis=0, keepdims=True)
         attend = jnp.exp(scores - top)
@@ -202,16 +208,14 @@
         both[h] = jnp.concatenate([kg[:, :NOPE], vg], axis=1)
         if h % 2 == 1:
             qrg[:, pl.ds((h - 1) * ROPE, 128)] = jnp.concatenate(rope_grads[-2:], axis=1)
-        if h == 0:
-            row_over(3)
-        if h < 3:
-            other_row_over(h + 1)
-        term = dot_nt(both[h], up)
-        latent_term = term if latent_term is None else latent_term + term
-        if h < 3:
-            if h > 0:
-                stage2(h - 1)
-            stage1(h)
+        up_before = up
+        if h > 0:
+            s1[h - 1] = push(ugb.at[h - 1, :, 1 - c], sb.at[h - 1], to_sib)
+        if h < 2:
+            other_row_over(h + 2)
+        if h > 1:
+            stage2(h - 2)
+    latent_term = latent_term + dot_nt(both[3], up_before)
 
     lgb[pl.ds(0, 3), :, :, pl.ds(0, LAT)] = latent_term[64:].reshape(3, NZ, 8, LAT)
     lgb[3, :, :, pl.ds(0, LAT)] = latent_term[:64].reshape(NZ, 8, LAT)
@@ -256,10 +260,10 @@
     outs = []
     stage1(3)
     stage2(2)
+    outs.append(on_device_copy(qng, qng_hbm))
+    outs.append(on_device_copy(qrg, qrg_hbm))
     stage3(0)
     stage2(3)
-    outs.append(on_device_copy(qng, qng_hbm))
-    outs.append(on_device_copy(qrg, qrg_hbm))
     stage3(1)
     latent_step2(0)
     stage3(2)

time: 66.9 us -> 66 us (0.987)
  Pallas kernels: 66 us -> 65 us
    pallas_call x1, Pallas kernels: 65.1 us -> 64.1 us  [on_device(): pl.pallas_call(kernel, out_shape=out_shape, in_specs=[hbm] * 5 + [pl.Bloc...]
where the time goes in v3:
time: 66 us; the launch traced here: 65.7 us
  Pallas kernels  65 us (98%)
    pallas_call x1, Pallas kernels, on_device(): pl.pallas_call(kernel, out_shape=out_shape, in_specs=[hbm] * 5 + [pl.Bloc...  64.1 us

profile of v3, /device:TPU:1, one launch (start us, length us, event | category | flops | bytes accessed | tf_op | source)
XLA Modules:
  0.0 65.7 jit_solution(7860518885044620344)
XLA Ops:
  0.6 64.1 %fused.1 = (f32[256,512]{1,0:T(8,128)S(1)}, f32[256,256]{1,0:T(8,128)S(1)}, f32[8,512]{1,0:T(8,128)S(1)}, f32[8,64]{1,0:T(8,128)S(1)}, f32[16,512]{1,0:T(8,128)S(1)}, /*index=5*/f32[16,512]{1,0:T(8,128)S(1)}) custom-call(f32[256,512]{1,0:T(8,128)} %qn_hbm.1, f32[256,256]{1,0:T(8,128)} %qr_hbm.1, f32[8,512]{1,0:T(8,128)} %lat_hbm.1, f32[8,64]{1,0:T(8,128)} %rk_hbm.1, ...), custom_call_target="tpu_custom_call" | custom-call | tf_op jit(solution)/shard_map/fused/pallas_call | solution.py:310
  64.7 0.9 %hand_over.1 = (f32[256,512]{1,0:T(8,128)}, f32[256,256]{1,0:T(8,128)}, f32[8,512]{1,0:T(8,128)}, f32[8,64]{1,0:T(8,128)}, f32[16,512]{1,0:T(8,128)}, /*index=5*/f32[16,512]{1,0:T(8,128)}) custom-call(f32[256,512]{1,0:T(8,128)S(1)} %get-tuple-element.12.refs_0_, f32[256,256]{1,0:T(8,128)S(1)} %get-tuple-element.13.refs_1_, ...), custom_call_target="tpu_custom_call" | custom-call | tf_op jit(solution)/shard_map/hand_over/pallas_call | solution.py:335
